TPU v7x, 32 devices: a whole 2x2x4 slice. The times are simulated.
32 devices in a mesh: gx: 8 (over z, core), gy: 4 (over y, x).
Axes of the slice: x: 2, y: 2, z: 4, core: 2. Of those that a mesh axis runs over, the one named last changes fastest.
Arguments:
- forcing: float32 [4, 8, 2048, 512], P(None, None, 'gx', 'gy'), may hold values from -150 to 150
- velocity: float32 [2, 2048, 512], P(None, 'gx', 'gy'), may hold values from -0.6 to 0.6
- viscosity: float32 [2048, 512], P('gx', 'gy'), may hold values from 0.05 to 0.25
- sound: float32 [2048, 512], P('gx', 'gy'), may hold values from 0.4 to 1
- coupling: float32 [4, 4, 2048, 512], P(None, None, 'gx', 'gy'), may hold values from -1.5 to 1.5
Outputs:
- basis: float32 [4, 8, 2048, 512], P(None, None, 'gx', 'gy')
- factor: float32 [8, 8], replicated
All inputs are finite; a program needn't handle non-finite values.
Results may differ from a plain program's by a relative error of at most 0.000055.
Values sent between devices are 32-bit elements; how exact they have to be, the bound alone decides.
A program may use at most 128 MiB of HBM per device.

v0:
```python
import jax
import jax.numpy as jnp
from jax import lax
from jax.sharding import PartitionSpec as P

STEP = 0.5


def with_halo(cells, sides, width):
    for axis, dim in sides:
        count = lax.axis_size(axis)
        ends = count - 1
        head = lax.slice_in_dim(cells, 0, width, axis=dim)
        tail = lax.slice_in_dim(cells, cells.shape[dim] - width, cells.shape[dim], axis=dim)
        cells = jnp.concatenate(
            [
                lax.ppermute(tail, axis, [(i, (i + 1) % count) for i in range(ends)]),
                cells,
                lax.ppermute(head, axis, [((i + 1) % count, i) for i in range(ends)]),
            ],
            axis=dim,
        )
    return cells


def tendency(padded, velocity, viscosity, sound, coupling):
    center = padded[:, :, 1:-1, 1:-1]
    east = padded[:, :, 2:, 1:-1]
    west = padded[:, :, :-2, 1:-1]
    north = padded[:, :, 1:-1, 2:]
    south = padded[:, :, 1:-1, :-2]
    grad_x = 0.5 * (east - west)
    grad_y = 0.5 * (north - south)
    laplace = east + west + north + south - 4.0 * center
    transport = viscosity * laplace - velocity[0] * grad_x - velocity[1] * grad_y
    divergence = grad_x[1] + grad_y[2]
    acoustic = jnp.stack(
        [-sound * divergence, -sound * grad_x[3], -sound * grad_y[3], -sound * divergence]
    )
    mixing = coupling[:, 0][:, None] * center[0][None]
    for inner in range(1, 4):
        mixing = mixing + coupling[:, inner][:, None] * center[inner][None]
    return transport + acoustic - mixing


def extend(state):
    return with_halo(state, (("gx", 2), ("gy", 3)), 1)


def local(forcing, velocity, viscosity, sound, coupling):
    first = tendency(extend(forcing), velocity, viscosity, sound, coupling) + forcing
    middle = forcing + STEP * first
    second = tendency(extend(middle), velocity, viscosity, sound, coupling) + forcing
    response = forcing + 0.5 * STEP * (first + second)
    rows_total = float(
        4 * forcing.shape[2] * forcing.shape[3] * lax.axis_size("gx") * lax.axis_size("gy")
    )
    local_gram = (
        jnp.einsum("vcxy,vdxy->cd", response, response, precision=lax.Precision.HIGHEST)
        / rows_total
    )
    lower = jnp.linalg.cholesky(lax.psum(local_gram, ("gx", "gy")))
    identity = jnp.eye(lower.shape[0], dtype=lower.dtype)
    inverse = lax.linalg.triangular_solve(lower, identity, left_side=True, lower=True)
    basis = jnp.einsum("cd,vdxy->vcxy", inverse, response, precision=lax.Precision.HIGHEST)
    return (basis, lower.T)


def solution(mesh):
    in_specs = (
        P(None, None, "gx", "gy"),
        P(None, "gx", "gy"),
        P("gx", "gy"),
        P("gx", "gy"),
        P(None, None, "gx", "gy"),
    )
    out_specs = (P(None, None, "gx", "gy"), P())
    return jax.shard_map(local, mesh=mesh, in_specs=in_specs, out_specs=out_specs, check_vma=False)
```

profile of v0, /device:TPU:0, one launch (start us, length us, event | category | flops | bytes accessed | tf_op | source)
XLA Modules:
  0.0 194.5 jit_solution(11511523097730281250)
XLA Ops:
  2.9 3.2 %collective-permute-start.1 = (f32[4,8,1,128]{3,1,2,0:T(8,128)S(1)}, f32[4,8,1,128]{3,1,2,0:T(8,128)S(1)}, u32[]{:S(2)}, u32[]{:S(2)}) collective-permute-start(f32[4,8,1,128]{3,1,2,0:T(8,128)S(1)} %bitcast.56), channel_id=1, source_target_pairs={{0,4},{4,8},{8,12},{12,16},{16,20},{20,24},{24,28},{1,5},{5,9},{9,... | collective-permute-start | bytes 49160 | tf_op jit(solution)/shard_map/ppermute | solution.py:17
  6.1 3.8 %slice_bitcast_fusion.7 = (f32[8,256,128]{2,1,0:T(8,128)}, f32[8,256,128]{2,1,0:T(8,128)S(1)}, f32[8,256,128]{2,1,0:T(8,128)}, f32[8,256,128]{2,1,0:T(8,128)}) fusion(f32[4,8,256,128]{3,2,1,0:T(8,128)} %param.5), kind=kLoop, calls=%fused_computation.51 | loop fusion | bytes 8388608 | tf_op jit(solution)/shard_map/mul | solution.py:40
  10.0 1.4 slice_bitcast_fusion.11
  11.4 5.4 %copy.76 = f32[4,8,256,128]{2,1,3,0:T(8,128)} copy(f32[4,8,256,128]{3,2,1,0:T(8,128)} %param.5) | data formatting | bytes 8388608 | tf_op args[0]
  17.6 2.0 %copy.50 = f32[4,8,1,128]{2,1,3,0:T(8,128)} copy(f32[4,8,1,128]{3,1,2,0:T(8,128)S(1)} %collective-permute-done.1) | data formatting | bytes 32768 | tf_op jit(solution)/shard_map/ppermute | solution.py:17
  19.5 1.6 pad_maximum_fusion.19
  21.1 5.4 %collective-permute-start.3 = (f32[4,8,258,1]{2,1,3,0:T(8,128)}, f32[4,8,258,1]{2,1,3,0:T(8,128)}, u32[]{:S(2)}, u32[]{:S(2)}) collective-permute-start(f32[4,8,258,1]{2,1,3,0:T(8,128)} %get-tuple-element.16), channel_id=1, source_target_pairs={{0,1},{1,2},{2,3},{4,5},{5,6},{6,7},{8,9},{9,10},{10,11},{12,13},{... | collective-permute-start | bytes 99080 | tf_op jit(solution)/shard_map/ppermute | solution.py:17
  27.9 1.4 copy.66
  30.5 2.6 %copy.64 = f32[8,256,128]{1,0,2:T(8,128)} copy(f32[8,256,128]{2,1,0:T(8,128)} %get-tuple-element.35) | data formatting | bytes 2097152 | tf_op jit(solution)/shard_map/mul | solution.py:42
  34.4 2.6 %copy.62 = f32[8,256,128]{1,0,2:T(8,128)} copy(f32[8,256,128]{2,1,0:T(8,128)} %get-tuple-element.34) | data formatting | bytes 2097152 | tf_op jit(solution)/shard_map/mul | solution.py:42
  37.0 2.0 %copy.61 = f32[4,256,128]{1,2,0:T(8,128)} copy(f32[4,256,128]{2,1,0:T(8,128)} %get-tuple-element.37) | data formatting | bytes 1048576 | tf_op jit(solution)/shard_map/mul | solution.py:42
  39.0 2.7 %copy.60 = f32[8,256,128]{1,0,2:T(8,128)} copy(f32[8,256,128]{2,1,0:T(8,128)} %get-tuple-element.32) | data formatting | bytes 2097152 | tf_op jit(solution)/shard_map/mul | solution.py:40
  41.7 2.0 %copy.59 = f32[4,256,128]{1,2,0:T(8,128)} copy(f32[4,256,128]{2,1,0:T(8,128)} %get-tuple-element.36) | data formatting | bytes 1048576 | tf_op jit(solution)/shard_map/mul | solution.py:40
  46.7 10.8 %fusion.8 = (f32[4,8,256,128]{2,1,3,0:T(8,128)S(1)}, f32[4,8,256,128]{2,1,3,0:T(8,128)S(1)}) fusion(f32[4,8,1,128]{2,1,3,0:T(8,128)S(1)} %copy.48, f32[4,8,256,128]{2,1,3,0:T(8,128)} %copy.76, f32[4,8,1,128]{2,1,3,0:T(8,128)} %copy.50, f32[4,8,258,1]{2,1,3,0:T(8,128)} %collective-permute-done.3, f32[4,8,258,1]{2,1,3,0:T(8,128)} %collective-permute-done.2), kind=kLoop, calls=%fused_computation.27 | loop fusion | flops 12582912 | bytes 12681728 | tf_op jit(solution)/shard_map/mul | solution.py:32
  57.6 1.9 slice_multiply_fusion.3
  61.5 11.5 %multiply_add_fusion = (f32[4,8,256,128]{2,1,3,0:T(8,128)S(1)}, f32[4,8,256,128]{2,1,3,0:T(8,128)}) fusion(f32[4,8,256,128]{2,1,3,0:T(8,128)S(1)} %copy-done.2, f32[8,256,128]{1,0,2:T(8,128)} %copy.66, f32[4,256,128]{1,2,0:T(8,128)S(1)} %copy.65, f32[8,256,128]{1,0,2:T(8,128)} %copy.64, f32[4,256,128]{1,2,0:T(8,128)S(1)} %copy.63, f32[8,256,128]{1,0,2:T(8,128)} %copy.62, ...), kind=kLoop, calls=%fused_computation.25 | loop fusion | flops 36700160 | bytes 22512128 | tf_op jit(solution)/shard_map/add | solution.py:52
  73.0 2.5 %fusion.18 = (f32[4,8,1,128]{2,1,3,0:T(8,128)S(1)}, f32[4,8,1,128]{2,1,3,0:T(8,128)}) fusion(f32[4,8,256,128]{2,1,3,0:T(8,128)S(1)} %get-tuple-element.8), kind=kLoop, calls=%fused_computation.74 | loop fusion | bytes 65536 | tf_op jit(solution)/shard_map/slice | solution.py:14
  75.7 2.2 %copy.69 = f32[4,8,1,128]{3,1,2,0:T(8,128)S(1)} copy(f32[4,8,1,128]{2,1,3,0:T(8,128)} %get-tuple-element.29) | data formatting | bytes 32768 | tf_op jit(solution)/shard_map/slice | solution.py:13
  80.5 4.0 %collective-permute-start.5 = (f32[4,8,1,128]{3,1,2,0:T(8,128)}, f32[4,8,1,128]{3,1,2,0:T(8,128)}, u32[]{:S(2)}, u32[]{:S(2)}) collective-permute-start(f32[4,8,1,128]{3,1,2,0:T(8,128)} %copy.71), channel_id=1, source_target_pairs={{0,4},{4,8},{8,12},{12,16},{16,20},{20,24},{24,28},{1,5},{5,9},{9,... | collective-permute-start | bytes 49160 | tf_op jit(solution)/shard_map/ppermute | solution.py:17
  85.9 2.8 %copy.72 = f32[4,8,1,128]{2,1,3,0:T(8,128)} copy(f32[4,8,1,128]{3,1,2,0:T(8,128)} %collective-permute-done.5) | data formatting | bytes 32768 | tf_op jit(solution)/shard_map/ppermute | solution.py:17
  89.7 4.4 %collective-permute-start.7 = (f32[4,8,258,1]{2,1,3,0:T(8,128)S(1)}, f32[4,8,258,1]{2,1,3,0:T(8,128)S(1)}, u32[]{:S(2)}, u32[]{:S(2)}) collective-permute-start(f32[4,8,258,1]{2,1,3,0:T(8,128)S(1)} %get-tuple-element.12), channel_id=1, source_target_pairs={{0,1},{1,2},{2,3},{4,5},{5,6},{6,7},{8,9},{9,10},{10,11},{12,13},{... | collective-permute-start | bytes 99080 | tf_op jit(solution)/shard_map/ppermute | solution.py:17
  94.1 1.6 collective-permute-start.6
  95.8 2.0 %slice_bitcast_fusion.3 = (f32[8,256,128]{1,0,2:T(8,128)}, f32[8,256,128]{1,0,2:T(8,128)}, f32[8,256,128]{1,0,2:T(8,128)}, f32[8,256,128]{1,0,2:T(8,128)}) fusion(f32[4,8,256,128]{2,1,3,0:T(8,128)S(1)} %copy-done.1), kind=kLoop, calls=%fused_computation.39 | loop fusion | bytes 8388608 | tf_op jit(solution)/shard_map/mul | solution.py:40
  97.8 3.0 %collective-permute-done.6 = f32[4,8,258,1]{2,1,3,0:T(8,128)S(1)} collective-permute-done((f32[4,8,258,1]{2,1,3,0:T(8,128)S(1)}, f32[4,8,258,1]{2,1,3,0:T(8,128)S(1)}, u32[]{:S(2)}, u32[]{:S(2)}) %collective-permute-start.6) | collective-permute-done | bytes 33056 | tf_op jit(solution)/shard_map/ppermute | solution.py:19
  100.8 6.9 %fusion.10 = (f32[4,8,256,128]{2,1,3,0:T(8,128)}, f32[4,8,256,128]{2,1,3,0:T(8,128)}) fusion(f32[4,8,1,128]{2,1,3,0:T(8,128)S(1)} %copy.70, f32[4,8,256,128]{2,1,3,0:T(8,128)S(1)} %copy-done.1, f32[4,8,1,128]{2,1,3,0:T(8,128)S(1)} %copy-done.5, f32[4,8,258,1]{2,1,3,0:T(8,128)S(1)} %collective-permute-done.7, f32[4,8,258,1]{2,1,3,0:T(8,128)S(1)} %collective-permute-done.6), kind=kLoop, calls=%fused_computation.29 | loop fusion | flops 12582912 | bytes 12681728 | tf_op jit(solution)/shard_map/mul | solution.py:32
  107.7 4.0 %slice_multiply_fusion.1 = (f32[1,8,256,128]{2,1,3,0:T(8,128)S(1)}, f32[1,8,256,128]{2,1,3,0:T(8,128)}, f32[1,8,256,128]{2,1,3,0:T(8,128)}) fusion(f32[4,8,256,128]{2,1,3,0:T(8,128)} %get-tuple-element.10, f32[256,128]{0,1:T(8,128)S(1)} %copy-done.11, f32[4,8,256,128]{2,1,3,0:T(8,128)} %get-tuple-element.11), kind=kLoop, calls=%fused_computation.41 | loop fusion | flops 1048576 | bytes 7471104 | tf_op jit(solution)/shard_map/mul | solution.py:38
  111.8 11.4 %fusion.6 = f32[4,8,256,128]{2,1,3,0:T(8,128)} fusion(f32[4,8,256,128]{2,1,3,0:T(8,128)S(1)} %copy-done.3, f32[4,8,256,128]{2,1,3,0:T(8,128)S(1)} %copy-done.6, f32[1,8,256,128]{2,1,3,0:T(8,128)} %get-tuple-element.19, f32[1,8,256,128]{2,1,3,0:T(8,128)} %get-tuple-element.20, f32[1,8,256,128]{2,1,3,0:T(8,128)S(1)} %get-tuple-element.18, ...), kind=kLoop, calls=%fused_computation.24 | loop fusion | flops 37748736 | bytes 26706432 | tf_op jit(solution)/shard_map/add | solution.py:54
  123.2 5.5 %copy.80 = f32[4,8,256,128]{3,1,2,0:T(8,128)} copy(f32[4,8,256,128]{2,1,3,0:T(8,128)} %fusion.6) | data formatting | bytes 8388608 | tf_op jit(solution)/shard_map/add | solution.py:54
  128.7 12.6 %fusion.11 = f32[8,8]{0,1:T(8,128)S(1)} fusion(f32[4,8,256,128]{2,1,3,0:T(8,128)} %fusion.6), kind=kOutput, calls=%fused_computation.35 | convolution fusion | flops 100663360 | bytes 4194560 | tf_op jit(solution)/shard_map/vcxy,vdxy->cd/dot_general | solution.py:59
  141.3 41.5 %psum.7 = f32[8,8]{0,1:T(8,128)S(1)} all-reduce(f32[8,8]{0,1:T(8,128)S(1)} %fusion.11), channel_id=1, replica_groups=mesh['gx'=8,'gy'=4] {'gx','gy'}, use_global_device_ids=true, to_apply=%region_0.0 | all-reduce | flops 64 | bytes 512 | tf_op jit(solution)/shard_map/psum | solution.py:62
  185.7 5.3 %convolution_bitcast_fusion = f32[4,8,256,128]{3,1,2,0:T(8,128)S(1)} fusion(f32[4,8,256,128]{3,1,2,0:T(8,128)} %copy.80, f32[8,8,1,1]{1,0,3,2:T(8,128)S(1)} %convolution_bitcast_fusion.1), kind=kOutput, calls=%fused_computation.30 | convolution fusion | flops 100663296 | bytes 8388864 | tf_op jit(solution)/shard_map/cd,vdxy->vcxy/dot_general | solution.py:65
  191.1 2.8 %copy.81 = f32[4,8,256,128]{3,2,1,0:T(8,128)} copy(f32[4,8,256,128]{3,1,2,0:T(8,128)S(1)} %convolution_bitcast_fusion) | data formatting | bytes 8388608
  (58 shorter events, 20.7 us)
Async XLA Ops:
  1.6 15.2 %collective-permute-start = (f32[4,8,1,128]{3,1,2,0:T(8,128)S(1)}, f32[4,8,1,128]{3,1,2,0:T(8,128)S(1)}, u32[]{:S(2)}, u32[]{:S(2)}) collective-permute-start(f32[4,8,1,128]{3,1,2,0:T(8,128)S(1)} %bitcast.57), channel_id=1, source_target_pairs={{4,0},{8,4},{12,8},{16,12},{20,16},{24,20},{28,24},{5,1},{9,5},{13... | collective-permute-start | bytes 49160 | tf_op jit(solution)/shard_map/ppermute | solution.py:19
  2.9 7.0 %copy-start.9 = (f32[4,4,256,128]{3,2,1,0:T(8,128)S(1)}, f32[4,4,256,128]{3,2,1,0:T(8,128)}, u32[]{:S(2)}) copy-start(f32[4,4,256,128]{3,2,1,0:T(8,128)} %param.9) | copy-start | bytes 6291460
  2.9 14.6 %collective-permute-start.1 = (f32[4,8,1,128]{3,1,2,0:T(8,128)S(1)}, f32[4,8,1,128]{3,1,2,0:T(8,128)S(1)}, u32[]{:S(2)}, u32[]{:S(2)}) collective-permute-start(f32[4,8,1,128]{3,1,2,0:T(8,128)S(1)} %bitcast.56), channel_id=1, source_target_pairs={{0,4},{4,8},{8,12},{12,16},{16,20},{20,24},{24,28},{1,5},{5,9},{9,... | collective-permute-start | bytes 49160 | tf_op jit(solution)/shard_map/ppermute | solution.py:17
  19.5 8.3 %copy-start.12 = (f32[2,256,128]{2,1,0:T(8,128)S(1)}, f32[2,256,128]{2,1,0:T(8,128)}, u32[]{:S(2)}) copy-start(f32[2,256,128]{2,1,0:T(8,128)} %param.6) | copy-start | bytes 786436
  21.1 25.6 %collective-permute-start.3 = (f32[4,8,258,1]{2,1,3,0:T(8,128)}, f32[4,8,258,1]{2,1,3,0:T(8,128)}, u32[]{:S(2)}, u32[]{:S(2)}) collective-permute-start(f32[4,8,258,1]{2,1,3,0:T(8,128)} %get-tuple-element.16), channel_id=1, source_target_pairs={{0,1},{1,2},{2,3},{4,5},{5,6},{6,7},{8,9},{9,10},{10,11},{12,13},{... | collective-permute-start | bytes 99080 | tf_op jit(solution)/shard_map/ppermute | solution.py:17
  26.6 20.1 %collective-permute-start.2 = (f32[4,8,258,1]{2,1,3,0:T(8,128)}, f32[4,8,258,1]{2,1,3,0:T(8,128)}, u32[]{:S(2)}, u32[]{:S(2)}) collective-permute-start(f32[4,8,258,1]{2,1,3,0:T(8,128)} %get-tuple-element.17), channel_id=1, source_target_pairs={{1,0},{2,1},{3,2},{5,4},{6,5},{7,6},{9,8},{10,9},{11,10},{13,12},{... | collective-permute-start | bytes 99080 | tf_op jit(solution)/shard_map/ppermute | solution.py:19
  46.7 10.9 %copy-start.10 = (f32[256,128]{0,1:T(8,128)S(1)}, f32[256,128]{0,1:T(8,128)}, u32[]{:S(2)}) copy-start(f32[256,128]{0,1:T(8,128)} %copy.58) | copy-start | bytes 393220
  57.5 3.3 %copy-start.2 = (f32[4,8,256,128]{2,1,3,0:T(8,128)S(1)}, f32[4,8,256,128]{2,1,3,0:T(8,128)}, u32[]{:S(2)}) copy-start(f32[4,8,256,128]{2,1,3,0:T(8,128)} %copy.76) | copy-start | bytes 12582916
  57.5 4.0 %copy-start.4 = (f32[4,8,1,128]{2,1,3,0:T(8,128)S(1)}, f32[4,8,1,128]{2,1,3,0:T(8,128)}, u32[]{:S(2)}) copy-start(f32[4,8,1,128]{2,1,3,0:T(8,128)} %copy.50) | copy-start | bytes 49156
  73.0 2.7 %copy-start = (f32[4,8,256,128]{2,1,3,0:T(8,128)}, f32[4,8,256,128]{2,1,3,0:T(8,128)S(1)}, u32[]{:S(2)}) copy-start(f32[4,8,256,128]{2,1,3,0:T(8,128)S(1)} %get-tuple-element.8) | copy-start | bytes 12582916
  77.9 6.6 %collective-permute-start.4 = (f32[4,8,1,128]{3,1,2,0:T(8,128)S(1)}, f32[4,8,1,128]{3,1,2,0:T(8,128)}, u32[]{:S(2)}, u32[]{:S(2)}) collective-permute-start(f32[4,8,1,128]{3,1,2,0:T(8,128)S(1)} %copy.69), channel_id=1, source_target_pairs={{4,0},{8,4},{12,8},{16,12},{20,16},{24,20},{28,24},{5,1},{9,5},{13... | collective-permute-start | bytes 49160 | tf_op jit(solution)/shard_map/ppermute | solution.py:19
  80.5 5.4 %collective-permute-start.5 = (f32[4,8,1,128]{3,1,2,0:T(8,128)}, f32[4,8,1,128]{3,1,2,0:T(8,128)}, u32[]{:S(2)}, u32[]{:S(2)}) collective-permute-start(f32[4,8,1,128]{3,1,2,0:T(8,128)} %copy.71), channel_id=1, source_target_pairs={{0,4},{4,8},{8,12},{12,16},{16,20},{20,24},{24,28},{1,5},{5,9},{9,... | collective-permute-start | bytes 49160 | tf_op jit(solution)/shard_map/ppermute | solution.py:17
  88.7 7.1 %copy-start.1 = (f32[4,8,256,128]{2,1,3,0:T(8,128)S(1)}, f32[4,8,256,128]{2,1,3,0:T(8,128)}, u32[]{:S(2)}) copy-start(f32[4,8,256,128]{2,1,3,0:T(8,128)} %copy-done) | copy-start | bytes 12582916
  89.7 8.1 %collective-permute-start.7 = (f32[4,8,258,1]{2,1,3,0:T(8,128)S(1)}, f32[4,8,258,1]{2,1,3,0:T(8,128)S(1)}, u32[]{:S(2)}, u32[]{:S(2)}) collective-permute-start(f32[4,8,258,1]{2,1,3,0:T(8,128)S(1)} %get-tuple-element.12), channel_id=1, source_target_pairs={{0,1},{1,2},{2,3},{4,5},{5,6},{6,7},{8,9},{9,10},{10,11},{12,13},{... | collective-permute-start | bytes 99080 | tf_op jit(solution)/shard_map/ppermute | solution.py:17
  94.1 6.6 %copy-start.5 = (f32[4,8,1,128]{2,1,3,0:T(8,128)S(1)}, f32[4,8,1,128]{2,1,3,0:T(8,128)}, u32[]{:S(2)}) copy-start(f32[4,8,1,128]{2,1,3,0:T(8,128)} %copy.72) | copy-start | bytes 49156
  94.1 6.6 %collective-permute-start.6 = (f32[4,8,258,1]{2,1,3,0:T(8,128)S(1)}, f32[4,8,258,1]{2,1,3,0:T(8,128)S(1)}, u32[]{:S(2)}, u32[]{:S(2)}) collective-permute-start(f32[4,8,258,1]{2,1,3,0:T(8,128)S(1)} %get-tuple-element.13), channel_id=1, source_target_pairs={{1,0},{2,1},{3,2},{5,4},{6,5},{7,6},{9,8},{10,9},{11,10},{13,12},{... | collective-permute-start | bytes 99080 | tf_op jit(solution)/shard_map/ppermute | solution.py:19
  97.8 9.9 %copy-start.11 = (f32[256,128]{0,1:T(8,128)S(1)}, f32[256,128]{0,1:T(8,128)}, u32[]{:S(2)}) copy-start(f32[256,128]{0,1:T(8,128)} %copy.58) | copy-start | bytes 393220
  100.8 10.9 %copy-start.6 = (f32[4,8,256,128]{2,1,3,0:T(8,128)S(1)}, f32[4,8,256,128]{2,1,3,0:T(8,128)}, u32[]{:S(2)}) copy-start(f32[4,8,256,128]{2,1,3,0:T(8,128)} %get-tuple-element.9) | copy-start | bytes 12582916
  107.7 4.0 %copy-start.3 = (f32[4,8,256,128]{2,1,3,0:T(8,128)S(1)}, f32[4,8,256,128]{2,1,3,0:T(8,128)}, u32[]{:S(2)}) copy-start(f32[4,8,256,128]{2,1,3,0:T(8,128)} %copy.76) | copy-start | bytes 12582916
  107.7 4.0 %copy-start.7 = (f32[4,256,128]{1,2,0:T(8,128)S(1)}, f32[4,256,128]{1,2,0:T(8,128)}, u32[]{:S(2)}) copy-start(f32[4,256,128]{1,2,0:T(8,128)} %copy.61) | copy-start | bytes 1572868
  107.7 4.1 %copy-start.8 = (f32[4,256,128]{1,2,0:T(8,128)S(1)}, f32[4,256,128]{1,2,0:T(8,128)}, u32[]{:S(2)}) copy-start(f32[4,256,128]{1,2,0:T(8,128)} %copy.59) | copy-start | bytes 1572868
where the time goes:
time: 196 us; the launch traced here: 195 us
  local copies, waits for them, and re-layouts  55.8 us (28%)
  other arithmetic  52.7 us (27%)
  blocking collectives  41.5 us (21%)
  starting transfers between devices  22.5 us (11%)
  matrix products  18.1 us (9%)
  waiting for transfers between devices  2.98 us (2%)
    psum x1, blocking collectives, local(): lower = jnp.linalg.cholesky(lax.psum(local_gram, ('gx', 'gy')))  41.5 us
    mul x2, other arithmetic, tendency(): grad_x = 0.5 * (east - west)  17.8 us
    ppermute x4, starting transfers between devices, with_halo(): lax.ppermute(tail, axis, [(i, (i + 1) % count) for i in range(ends)])  17 us
    dot_general x1, matrix products, local(): jnp.einsum('vcxy,vdxy->cd', response, response, precision=lax.Precision.H...  12.6 us
    unnamed x30, local copies, waits for them, and re-layouts  12.3 us
    mul x5, local copies, waits for them, and re-layouts, tendency(): mixing = coupling[:, 0][:, None] * center[0][None]  12.1 us
    add x1, other arithmetic, local(): middle = forcing + STEP * first  11.5 us
    add x1, other arithmetic, local(): response = forcing + 0.5 * STEP * (first + second)  11.4 us
  transfers between devices with their start and end apart: 8, of which 1 were waited for; matrix products, arithmetic and copies ran while one was open for 18% of the time, Pallas kernels for 0%

commit v1 on v0

v1 whole, which is shorter than its diff:
```python
import functools

import jax
import jax.numpy as jnp
from jax import lax
from jax.experimental import pallas as pl
from jax.experimental.pallas import tpu as pltpu
from jax.sharding import PartitionSpec as P

MESH = pl.DeviceIdType.MESH
NV = 4
NC = 8
GROUPS = 2
CG = NC // GROUPS
NF = NV * CG
PAIRS = [(i, j) for i in range(NC) for j in range(i + 1)]
PAIR_INDEX = {p: k for k, p in enumerate(PAIRS)}
PADDED_PAIRS = 40
KE, KW, KN, KS, KA, KM = 0, 1, 2, 3, 4, 5
KD = KM + NV * NV
NK = KD + NV


def response_kernel(
    nx, ny, f_hbm, vel_hbm, visc_hbm, sound_hbm, coup_hbm,
    r_hbm, gram_ref,
    fbuf, mbuf, rbuf, coef, halo, pack, tpose,
    vel, visc, sound, coup, acc, gx_slots, gy_slots,
    row_send, row_recv, col_send, col_recv,
    in_sem, out_sem, rs_sem, rr_sem, cs_sem, cr_sem, g1_send, g1_recv, g2_send, g2_recv,
):
    rows = f_hbm.shape[2]
    chunks = rows // 8
    halves = rows // 128
    gx, gy = lax.axis_index("gx"), lax.axis_index("gy")

    def cols(ref, g):
        return ref.at[:, pl.ds(g * CG, CG)]

    loads = []
    for g in range(GROUPS):
        loads.append(pltpu.make_async_copy(
            cols(f_hbm, g), fbuf.at[:, pl.ds(g * CG, CG), pl.ds(8, rows)], in_sem.at[g]))
    coef_loads = [
        pltpu.make_async_copy(a, b, in_sem.at[GROUPS + k])
        for k, (a, b) in enumerate(
            [(vel_hbm, vel), (visc_hbm, visc), (sound_hbm, sound), (coup_hbm, coup)])
    ]
    for cp in loads + coef_loads:
        cp.start()

    barrier = pltpu.get_barrier_semaphore()
    for r in range(1, nx):
        pl.semaphore_signal(barrier, inc=1, device_id=(lax.rem(gx + r, nx), gy), device_id_type=MESH)
    for r in range(1, ny):
        pl.semaphore_signal(barrier, inc=1, device_id=(gx, lax.rem(gy + r, ny)), device_id_type=MESH)

    def zero_side(ref, side):
        for s in range(2):
            for g in range(GROUPS):
                ref[s, g, side] = jnp.zeros(ref.shape[3:], jnp.float32)

    pl.when(gx == 0)(lambda: zero_side(row_recv, 0))
    pl.when(gx == nx - 1)(lambda: zero_side(row_recv, 1))
    pl.when(gy == 0)(lambda: zero_side(col_recv, 0))
    pl.when(gy == ny - 1)(lambda: zero_side(col_recv, 1))

    lane = lax.broadcasted_iota(jnp.int32, (8, 128), 1)
    first_lane = lane == 0
    last_lane = lane == 127

    def row_copy(s, g, up):
        return pltpu.make_async_remote_copy(
            src_ref=row_send.at[s, g, up], dst_ref=row_recv.at[s, g, 1 - up],
            send_sem=rs_sem.at[s, g, up], recv_sem=rr_sem.at[s, g, 1 - up],
            device_id=(gx + (1 if up else -1), gy), device_id_type=MESH)

    def col_copy(s, g, up):
        return pltpu.make_async_remote_copy(
            src_ref=col_send.at[s, g, up], dst_ref=col_recv.at[s, g, 1 - up],
            send_sem=cs_sem.at[s, g, up], recv_sem=cr_sem.at[s, g, 1 - up],
            device_id=(gx, gy + (1 if up else -1)), device_id_type=MESH)

    def send(s, g, src):
        for v in range(NV):
            for cl in range(CG):
                k = v * CG + cl
                row_send[s, g, 0, k:k + 1, :] = src[v, g * CG + cl, 8:9, :]
                row_send[s, g, 1, k:k + 1, :] = src[v, g * CG + cl, 7 + rows:8 + rows, :]
        for h in range(halves):
            tpose[...] = pack[h * 128:(h + 1) * 128, :].T
            col_send[s, g, 1, h * NF:(h + 1) * NF, :] = tpose[pl.ds(0, NF, stride=2), :]
            col_send[s, g, 0, h * NF:(h + 1) * NF, :] = tpose[pl.ds(1, NF, stride=2), :]

    def launch(s, g):
        pl.when(gx > 0)(lambda: row_copy(s, g, 0).start())
        pl.when(gx < nx - 1)(lambda: row_copy(s, g, 1).start())
        pl.when(gy > 0)(lambda: col_copy(s, g, 0).start())
        pl.when(gy < ny - 1)(lambda: col_copy(s, g, 1).start())

    def receive(s, g, dst):
        pl.when(gx > 0)(lambda: row_copy(s, g, 1).wait_recv())
        pl.when(gx < nx - 1)(lambda: row_copy(s, g, 0).wait_recv())
        pl.when(gy > 0)(lambda: col_copy(s, g, 1).wait_recv())
        pl.when(gy < ny - 1)(lambda: col_copy(s, g, 0).wait_recv())
        for v in range(NV):
            for cl in range(CG):
                k = v * CG + cl
                dst[v, g * CG + cl, 7:8, :] = row_recv[s, g, 0, k:k + 1, :]
                dst[v, g * CG + cl, 8 + rows:9 + rows, :] = row_recv[s, g, 1, k:k + 1, :]
        for h in range(halves):
            tpose[pl.ds(0, NF, stride=2), :] = col_recv[s, g, 1, h * NF:(h + 1) * NF, :]
            tpose[pl.ds(1, NF, stride=2), :] = col_recv[s, g, 0, h * NF:(h + 1) * NF, :]
            halo[h * 128:(h + 1) * 128, :] = tpose[...].T

    def finish_sends(s, g):
        pl.when(gx > 0)(lambda: row_copy(s, g, 0).wait_send())
        pl.when(gx < nx - 1)(lambda: row_copy(s, g, 1).wait_send())
        pl.when(gy > 0)(lambda: col_copy(s, g, 0).wait_send())
        pl.when(gy < ny - 1)(lambda: col_copy(s, g, 1).wait_send())

    def packed(total, value, k):
        return jnp.where((lane == 2 * k) | (lane == 2 * k + 1), pltpu.roll(value, 2 * k + 1, 1), total)

    def pack_input(g):
        def body(i, _):
            at = pl.multiple_of(i * 8, 8)
            total = jnp.zeros((8, 128), jnp.float32)
            for v in range(NV):
                for cl in range(CG):
                    value = fbuf[v, g * CG + cl, pl.ds(at + 8, 8), :]
                    total = packed(total, value, v * CG + cl)
            pack[pl.ds(at, 8), :] = total
            return 0
        lax.fori_loop(0, chunks, body, 0, unroll=4)

    def operator(src, g, cl, at, ks, edges, first):
        q, d1, d2, out = [], {}, {}, []
        for v in range(NV):
            c = g * CG + cl
            mid = src[v, c, pl.ds(at + 8, 8), :]
            east = src[v, c, pl.ds(at + 9, 8), :]
            west = src[v, c, pl.ds(at + 7, 8), :]
            edge = pltpu.roll(edges, 127 - 2 * (v * CG + cl), 1)
            north = jnp.where(last_lane, edge, pltpu.roll(mid, 127, 1))
            south = jnp.where(first_lane, edge, pltpu.roll(mid, 1, 1))
            q.append(mid)
            if v in (1, 3):
                d1[v] = east - west
            if v in (2, 3):
                d2[v] = north - south
            out.append((ks[KE] * east + ks[KW] * west) + (ks[KN] * north + ks[KS] * south))
        for w in range(NV):
            m = [ks[KD + v if first and v == w else KM + w * NV + v] * q[v] for v in range(NV)]
            out[w] = out[w] + ((m[0] + m[1]) + (m[2] + m[3]))
        div = ks[KA] * (d1[1] + d2[2])
        out[0] = out[0] - div
        out[1] = out[1] - ks[KA] * d1[3]
        out[2] = out[2] - ks[KA] * d2[3]
        out[3] = out[3] - div
        return out

    def stage_one(g):
        def body(i, _):
            at = pl.multiple_of(i * 8, 8)
            ks = [coef[k, pl.ds(at, 8), :] for k in range(NK)]
            edges = halo[pl.ds(at, 8), :]
            total = jnp.zeros((8, 128), jnp.float32)
            for cl in range(CG):
                middle = operator(fbuf, g, cl, at, ks, edges, True)
                for v in range(NV):
                    mbuf[v, g * CG + cl, pl.ds(at + 8, 8), :] = middle[v]
                    total = packed(total, middle[v], v * CG + cl)
            pack[pl.ds(at, 8), :] = total
            return 0
        lax.fori_loop(0, chunks, body, 0, unroll=2)

    def stage_two(g):
        def body(i, _):
            at = pl.multiple_of(i * 8, 8)
            ks = [coef[k, pl.ds(at, 8), :] for k in range(NK)]
            edges = halo[pl.ds(at, 8), :]
            res = {}
            for cl in range(CG):
                c = g * CG + cl
                out = operator(mbuf, g, cl, at, ks, edges, False)
                for v in range(NV):
                    value = 1.5 * fbuf[v, c, pl.ds(at + 8, 8), :] + out[v]
                    rbuf[v, c, pl.ds(at, 8), :] = value
                    res[v, c] = value
            for c in range(g * CG):
                for v in range(NV):
                    res[v, c] = rbuf[v, c, pl.ds(at, 8), :]
            for c in range(g * CG, (g + 1) * CG):
                for d in range(c + 1):
                    p = [res[v, c] * res[v, d] for v in range(NV)]
                    acc[PAIR_INDEX[c, d]] += (p[0] + p[1]) + (p[2] + p[3])
            return 0
        lax.fori_loop(0, chunks, body, 0, unroll=2)

    def r_copy(g):
        return pltpu.make_async_copy(cols(rbuf, g), cols(r_hbm, g), out_sem.at[g])

    for g in range(GROUPS):
        loads[g].wait()
        pack_input(g)
        send(0, g, fbuf)
        if g == 0:
            pl.semaphore_wait(barrier, nx + ny - 2)
        launch(0, g)
    acc[...] = jnp.zeros_like(acc)
    for cp in coef_loads:
        cp.wait()

    def fold(i, _):
        at = pl.multiple_of(i * 8, 8)
        half = 0.5 * visc[pl.ds(at, 8), :]
        vx = 0.25 * vel[0, pl.ds(at, 8), :]
        vy = 0.25 * vel[1, pl.ds(at, 8), :]
        coef[KE, pl.ds(at, 8), :] = half - vx
        coef[KW, pl.ds(at, 8), :] = half + vx
        coef[KN, pl.ds(at, 8), :] = half - vy
        coef[KS, pl.ds(at, 8), :] = half + vy
        coef[KA, pl.ds(at, 8), :] = 0.25 * sound[pl.ds(at, 8), :]
        for w in range(NV):
            for v in range(NV):
                k = -0.5 * coup[w, v, pl.ds(at, 8), :]
                if v == w:
                    coef[KD + v, pl.ds(at, 8), :] = k + (1.5 - 4.0 * half)
                    k = k + (1.0 - 4.0 * half)
                coef[KM + w * NV + v, pl.ds(at, 8), :] = k
        return 0
    lax.fori_loop(0, chunks, fold, 0)

    for g in range(GROUPS):
        receive(0, g, fbuf)
        stage_one(g)
        send(1, g, mbuf)
        launch(1, g)
    for g in range(GROUPS):
        receive(1, g, mbuf)
        stage_two(g)
        r_copy(g).start()

    scale = 0.25 / float(NV * rows * 128 * nx * ny)
    lanes = jnp.sum(jnp.sum(acc[...], axis=1), axis=1, keepdims=True)
    spot = lax.broadcasted_iota(jnp.int32, (PADDED_PAIRS, 128), 1) == lax.broadcasted_iota(
        jnp.int32, (PADDED_PAIRS, 128), 0)
    line = jnp.sum(jnp.where(spot, lanes, 0.0), axis=0, keepdims=True) * scale
    gx_slots[gx] = jnp.broadcast_to(line, (8, 128))

    def gx_copy(r, owner):
        return pltpu.make_async_remote_copy(
            src_ref=gx_slots.at[owner], dst_ref=gx_slots.at[owner],
            send_sem=g1_send.at[r], recv_sem=g1_recv.at[owner],
            device_id=(lax.rem(gx + r, nx), gy), device_id_type=MESH)

    def gy_copy(r, owner):
        return pltpu.make_async_remote_copy(
            src_ref=gy_slots.at[owner], dst_ref=gy_slots.at[owner],
            send_sem=g2_send.at[r], recv_sem=g2_recv.at[owner],
            device_id=(gx, lax.rem(gy + r, ny)), device_id_type=MESH)

    for r in range(1, nx):
        gx_copy(r, gx).start()
    for r in range(1, nx):
        gx_copy(r, lax.rem(gx + nx - r, nx)).wait_recv()
    gy_slots[gy] = functools.reduce(jnp.add, [gx_slots[k] for k in range(nx)])
    for r in range(1, ny):
        gy_copy(r, gy).start()
    for r in range(1, ny):
        gy_copy(r, lax.rem(gy + ny - r, ny)).wait_recv()
    gram_ref[...] = functools.reduce(jnp.add, [gy_slots[k] for k in range(ny)])

    for r in range(1, nx):
        gx_copy(r, gx).wait_send()
    for r in range(1, ny):
        gy_copy(r, gy).wait_send()
    for s in range(2):
        for g in range(GROUPS):
            finish_sends(s, g)
    for g in range(GROUPS):
        r_copy(g).wait()


def basis_kernel(gram_ref, r_ref, basis_ref, factor_ref, inv_ref):
    @pl.when((pl.program_id(0) == 0) & (pl.program_id(1) == 0))
    def _():
        gram = {p: jnp.broadcast_to(gram_ref[:, k:k + 1], (8, 128)) for k, p in enumerate(PAIRS)}
        low, inv, diag = {}, {}, {}
        for j in range(NC):
            for i in range(j, NC):
                s = gram[i, j]
                for k in range(j):
                    s = s - low[i, k] * low[j, k]
                if i == j:
                    r = lax.rsqrt(s)
                    r = r * (1.5 - 0.5 * s * r * r)
                    diag[j] = r
                    low[j, j] = s * r
                else:
                    low[i, j] = s * diag[j]
        for j in range(NC):
            inv[j, j] = diag[j]
            for i in range(j + 1, NC):
                s = low[i, j] * inv[j, j]
                for k in range(j + 1, i):
                    s = s + low[i, k] * inv[k, j]
                inv[i, j] = -diag[i] * s
        row = lax.broadcasted_iota(jnp.int32, (8, 128), 0)
        lane = lax.broadcasted_iota(jnp.int32, (8, 128), 1)
        factor = jnp.zeros((8, 128), jnp.float32)
        for k, (i, j) in enumerate(PAIRS):
            factor = jnp.where((row == j) & (lane == i), low[i, j], factor)
            inv_ref[k] = 0.5 * inv[i, j]
        factor_ref[...] = factor[:, :NC]

    inv = [inv_ref[k] for k in range(len(PAIRS))]

    def body(i, _):
        at = pl.multiple_of(i * 8, 8)
        r = [r_ref[0, c, pl.ds(at, 8), :] for c in range(NC)]
        for c in range(NC):
            total = inv[PAIR_INDEX[c, 0]] * r[0]
            for d in range(1, c + 1):
                total = total + inv[PAIR_INDEX[c, d]] * r[d]
            basis_ref[0, c, pl.ds(at, 8), :] = total
        return 0
    lax.fori_loop(0, r_ref.shape[2] // 8, body, 0, unroll=2)


def local(nx, ny, forcing, velocity, viscosity, sound, coupling):
    rows = forcing.shape[2]
    f32 = jnp.float32
    hbm = pl.BlockSpec(memory_space=pl.ANY)
    vmem = pl.BlockSpec(memory_space=pltpu.VMEM)
    dma = pltpu.SemaphoreType.DMA
    response, gram = pl.pallas_call(
        functools.partial(response_kernel, nx, ny),
        out_shape=(jax.ShapeDtypeStruct(forcing.shape, f32), jax.ShapeDtypeStruct((8, 128), f32)),
        in_specs=[pl.BlockSpec(memory_space=pltpu.HBM)] * 5,
        out_specs=(hbm, vmem),
        scratch_shapes=[
            pltpu.VMEM((NV, NC, rows + 16, 128), f32),
            pltpu.VMEM((NV, NC, rows + 16, 128), f32),
            pltpu.VMEM((NV, NC, rows, 128), f32),
            pltpu.VMEM((NK, rows, 128), f32),
            pltpu.VMEM((rows, 128), f32),
            pltpu.VMEM((rows, 128), f32),
            pltpu.VMEM((128, 128), f32),
            pltpu.VMEM(velocity.shape, f32),
            pltpu.VMEM(viscosity.shape, f32),
            pltpu.VMEM(sound.shape, f32),
            pltpu.VMEM(coupling.shape, f32),
            pltpu.VMEM((PADDED_PAIRS, 8, 128), f32),
            pltpu.VMEM((nx, 8, 128), f32),
            pltpu.VMEM((ny, 8, 128), f32),
            pltpu.VMEM((2, GROUPS, 2, NF, 128), f32),
            pltpu.VMEM((2, GROUPS, 2, NF, 128), f32),
            pltpu.VMEM((2, GROUPS, 2, rows // 128 * NF, 128), f32),
            pltpu.VMEM((2, GROUPS, 2, rows // 128 * NF, 128), f32),
            dma((GROUPS + 4,)), dma((GROUPS,)),
            dma((2, GROUPS, 2)), dma((2, GROUPS, 2)), dma((2, GROUPS, 2)), dma((2, GROUPS, 2)),
            dma((nx,)), dma((nx,)), dma((ny,)), dma((ny,)),
        ],
        compiler_params=pltpu.CompilerParams(
            collective_id=0, has_side_effects=True, vmem_limit_bytes=40 * 2**20),
        name="response",
    )(forcing, velocity, viscosity, sound, coupling)
    block = pl.BlockSpec((1, NC, rows // 2, 128), lambda v, i: (v, 0, i, 0))
    return tuple(pl.pallas_call(
        basis_kernel,
        grid=(NV, 2),
        out_shape=(jax.ShapeDtypeStruct(forcing.shape, f32), jax.ShapeDtypeStruct((NC, NC), f32)),
        in_specs=[pl.BlockSpec((8, 128), lambda v, i: (0, 0)), block],
        out_specs=(block, pl.BlockSpec((NC, NC), lambda v, i: (0, 0))),
        scratch_shapes=[pltpu.VMEM((len(PAIRS), 8, 128), f32)],
        compiler_params=pltpu.CompilerParams(vmem_limit_bytes=16 * 2**20),
        name="basis",
    )(gram, response))


def solution(mesh):
    in_specs = (
        P(None, None, "gx", "gy"),
        P(None, "gx", "gy"),
        P("gx", "gy"),
        P("gx", "gy"),
        P(None, None, "gx", "gy"),
    )
    out_specs = (P(None, None, "gx", "gy"), P())
    body = functools.partial(local, mesh.shape["gx"], mesh.shape["gy"])
    return jax.shard_map(body, mesh=mesh, in_specs=in_specs, out_specs=out_specs, check_vma=False)
```

time: 196 us -> 45.3 us (0.23)
  other arithmetic: 52.7 us -> 0 us
  local copies, waits for them, and re-layouts: 55.8 us -> 6.53 us
  blocking collectives: 41.5 us -> 0 us
  Pallas kernels: 0 us -> 37.9 us
  starting transfers between devices: 22.5 us -> 0 us
  matrix products: 18.1 us -> 0 us
  waiting for transfers between devices: 2.98 us -> 0 us
    psum x1 -> x0, blocking collectives: 41.5 us -> none  [local(): lower = jnp.linalg.cholesky(lax.psum(local_gram, ('gx', 'gy')))]
    pallas_call x0 -> x2, Pallas kernels: none -> 37.9 us  [the longest x1 33.3 us: local(): pl.pallas_call(functools.partial(response_kernel, nx, ny), out_shape=(jax...]
    mul x5 -> x0, other arithmetic: 23.7 us -> none  [the longest x2 17.8 us: tendency(): grad_x = 0.5 * (east - west)]
    mul x13 -> x0, local copies, waits for them, and re-layouts: 23.4 us -> none  [the longest x5 12.1 us: tendency(): mixing = coupling[:, 0][:, None] * center[0][None]]
    add x2 -> x0, other arithmetic: 22.9 us -> none  [the longest x1 11.5 us: local(): middle = forcing + STEP * first]
    ppermute x8 -> x0, starting transfers between devices: 22.5 us -> none  [the longest x4 17 us: with_halo(): lax.ppermute(tail, axis, [(i, (i + 1) % count) for i in range(ends)])]
    dot_general x2 -> x0, matrix products: 17.9 us -> none  [the longest x1 12.6 us: local(): jnp.einsum('vcxy,vdxy->cd', response, response, precision=lax.Precision.H...]
    slice x4 -> x0, local copies, waits for them, and re-layouts: 6.93 us -> none  [the longest x3 4.72 us: with_halo(): lax.slice_in_dim(cells, cells.shape[dim] - width, cells.shape[dim], axis=...]
  transfers between devices with their start and end apart: 8 -> 0, of which waited for: 1 -> 0; matrix products, arithmetic and copies ran while one was open for 18% -> 0% of each run, Pallas kernels for 0% -> 0%
where the time goes in v1:
time: 45.3 us; the launch traced here: 45.1 us
  Pallas kernels  37.9 us (84%)
  local copies, waits for them, and re-layouts  6.53 us (14%)
  between operations  0.65 us (1%)
    pallas_call x1, Pallas kernels, local(): pl.pallas_call(functools.partial(response_kernel, nx, ny), out_shape=(jax...  33.3 us
    unnamed x10, local copies, waits for them, and re-layouts  6.53 us
    pallas_call x1, Pallas kernels, local(): pl.pallas_call(basis_kernel, grid=(NV, 2), out_shape=(jax.ShapeDtypeStruc...  4.57 us

profile of v1, /device:TPU:0, one launch (start us, length us, event | category | flops | bytes accessed | tf_op | source)
XLA Modules:
  0.0 45.1 jit_solution(18319138709466800143)
XLA Ops:
  0.6 0.0 copy-start
  0.6 2.2 %copy-done = f32[4,8,256,128]{3,2,1,0:T(8,128)S(1)} copy-done((f32[4,8,256,128]{3,2,1,0:T(8,128)S(1)}, f32[4,8,256,128]{3,2,1,0:T(8,128)}, u32[]{:S(2)}) %copy-start) | copy-done | bytes 4194328
  2.8 0.0 copy-start.1
  2.8 1.6 %copy-done.1 = f32[4,4,256,128]{3,2,1,0:T(8,128)S(1)} copy-done((f32[4,4,256,128]{3,2,1,0:T(8,128)S(1)}, f32[4,4,256,128]{3,2,1,0:T(8,128)}, u32[]{:S(2)}) %copy-start.1) | copy-done | bytes 2097176
  4.4 0.0 copy-start.2
  4.4 0.9 %copy-done.2 = f32[2,256,128]{2,1,0:T(8,128)S(1)} copy-done((f32[2,256,128]{2,1,0:T(8,128)S(1)}, f32[2,256,128]{2,1,0:T(8,128)}, u32[]{:S(2)}) %copy-start.2) | copy-done | bytes 262168
  5.4 0.0 copy-start.3
  5.4 0.9 %copy-done.3 = f32[256,128]{1,0:T(8,128)S(1)} copy-done((f32[256,128]{1,0:T(8,128)S(1)}, f32[256,128]{1,0:T(8,128)}, u32[]{:S(2)}) %copy-start.3) | copy-done | bytes 131096
  6.3 0.0 copy-start.4
  6.3 0.9 %copy-done.4 = f32[256,128]{1,0:T(8,128)S(1)} copy-done((f32[256,128]{1,0:T(8,128)S(1)}, f32[256,128]{1,0:T(8,128)}, u32[]{:S(2)}) %copy-start.4) | copy-done | bytes 131096
  7.2 33.3 %response.1 = (f32[4,8,256,128]{3,2,1,0:T(8,128)S(1)}, f32[8,128]{1,0:T(8,128)S(1)}) custom-call(f32[4,8,256,128]{3,2,1,0:T(8,128)S(1)} %copy-done, f32[2,256,128]{2,1,0:T(8,128)S(1)} %copy-done.2, f32[256,128]{1,0:T(8,128)S(1)} %copy-done.3, f32[256,128]{1,0:T(8,128)S(1)} %copy-done.4, f32[4,4,256,128]{3,2,1,0:T(8,128)S(1)} %copy-done.1), custom_call_target="tpu_custom_call" | custom-call | tf_op jit(solution)/shard_map/response/pallas_call | solution.py:338
  40.5 4.6 %basis.1 = (f32[4,8,256,128]{3,2,1,0:T(8,128)}, f32[8,8]{1,0:T(8,128)}) custom-call(f32[8,128]{1,0:T(8,128)S(1)} %get-tuple-element.4.gram_ref, f32[4,8,256,128]{3,2,1,0:T(8,128)S(1)} %get-tuple-element.5.r_ref), custom_call_target="tpu_custom_call" | custom-call | tf_op jit(solution)/shard_map/basis/pallas_call | solution.py:371
Async XLA Ops:
  0.6 2.2 %copy-start = (f32[4,8,256,128]{3,2,1,0:T(8,128)S(1)}, f32[4,8,256,128]{3,2,1,0:T(8,128)}, u32[]{:S(2)}) copy-start(f32[4,8,256,128]{3,2,1,0:T(8,128)} %f_hbm.1) | copy-start | bytes 12582916
  2.8 1.6 %copy-start.1 = (f32[4,4,256,128]{3,2,1,0:T(8,128)S(1)}, f32[4,4,256,128]{3,2,1,0:T(8,128)}, u32[]{:S(2)}) copy-start(f32[4,4,256,128]{3,2,1,0:T(8,128)} %coup_hbm.1) | copy-start | bytes 6291460
  4.4 0.9 %copy-start.2 = (f32[2,256,128]{2,1,0:T(8,128)S(1)}, f32[2,256,128]{2,1,0:T(8,128)}, u32[]{:S(2)}) copy-start(f32[2,256,128]{2,1,0:T(8,128)} %vel_hbm.1) | copy-start | bytes 786436
  5.4 0.9 %copy-start.3 = (f32[256,128]{1,0:T(8,128)S(1)}, f32[256,128]{1,0:T(8,128)}, u32[]{:S(2)}) copy-start(f32[256,128]{1,0:T(8,128)} %visc_hbm.1) | copy-start | bytes 393220
  6.3 0.9 %copy-start.4 = (f32[256,128]{1,0:T(8,128)S(1)}, f32[256,128]{1,0:T(8,128)}, u32[]{:S(2)}) copy-start(f32[256,128]{1,0:T(8,128)} %sound_hbm.1) | copy-start | bytes 393220

commit v2 on v1

--- a/solution.py
+++ b/solution.py
@@ -230,7 +230,7 @@
                     k = k + (1.0 - 4.0 * half)
                 coef[KM + w * NV + v, pl.ds(at, 8), :] = k
         return 0
-    lax.fori_loop(0, chunks, fold, 0)
+    lax.fori_loop(0, chunks, fold, 0, unroll=2)
 
     for g in range(GROUPS):
         receive(0, g, fbuf)
@@ -283,9 +283,8 @@
         r_copy(g).wait()
 
 
-def basis_kernel(gram_ref, r_ref, basis_ref, factor_ref, inv_ref):
-    @pl.when((pl.program_id(0) == 0) & (pl.program_id(1) == 0))
-    def _():
+def basis_kernel(gram_ref, r_ref, basis_hbm, factor_ref, inv_ref, basis_ref, out_sem):
+    def factorise():
         gram = {p: jnp.broadcast_to(gram_ref[:, k:k + 1], (8, 128)) for k, p in enumerate(PAIRS)}
         low, inv, diag = {}, {}, {}
         for j in range(NC):
@@ -315,18 +314,26 @@
             inv_ref[k] = 0.5 * inv[i, j]
         factor_ref[...] = factor[:, :NC]
 
+    factorise()
     inv = [inv_ref[k] for k in range(len(PAIRS))]
 
-    def body(i, _):
-        at = pl.multiple_of(i * 8, 8)
-        r = [r_ref[0, c, pl.ds(at, 8), :] for c in range(NC)]
-        for c in range(NC):
-            total = inv[PAIR_INDEX[c, 0]] * r[0]
-            for d in range(1, c + 1):
-                total = total + inv[PAIR_INDEX[c, d]] * r[d]
-            basis_ref[0, c, pl.ds(at, 8), :] = total
-        return 0
-    lax.fori_loop(0, r_ref.shape[2] // 8, body, 0, unroll=2)
+    def out_copy(v):
+        return pltpu.make_async_copy(basis_ref.at[v], basis_hbm.at[v], out_sem.at[v])
+
+    for v in range(NV):
+        def body(i, _):
+            at = pl.multiple_of(i * 8, 8)
+            r = [r_ref[v, c, pl.ds(at, 8), :] for c in range(NC)]
+            for c in range(NC):
+                total = inv[PAIR_INDEX[c, 0]] * r[0]
+                for d in range(1, c + 1):
+                    total = total + inv[PAIR_INDEX[c, d]] * r[d]
+                basis_ref[v, c, pl.ds(at, 8), :] = total
+            return 0
+        lax.fori_loop(0, r_ref.shape[2] // 8, body, 0, unroll=2)
+        out_copy(v).start()
+    for v in range(NV):
+        out_copy(v).wait()
 
 
 def local(nx, ny, forcing, velocity, viscosity, sound, coupling):
@@ -366,15 +373,18 @@
         compiler_params=pltpu.CompilerParams(
             collective_id=0, has_side_effects=True, vmem_limit_bytes=40 * 2**20),
         name="response",
-    )(forcing, velocity, viscosity, sound, coupling)
-    block = pl.BlockSpec((1, NC, rows // 2, 128), lambda v, i: (v, 0, i, 0))
+    )(*[pltpu.with_memory_space_constraint(a, pltpu.HBM)
+        for a in (forcing, velocity, viscosity, sound, coupling)])
     return tuple(pl.pallas_call(
         basis_kernel,
-        grid=(NV, 2),
         out_shape=(jax.ShapeDtypeStruct(forcing.shape, f32), jax.ShapeDtypeStruct((NC, NC), f32)),
-        in_specs=[pl.BlockSpec((8, 128), lambda v, i: (0, 0)), block],
-        out_specs=(block, pl.BlockSpec((NC, NC), lambda v, i: (0, 0))),
-        scratch_shapes=[pltpu.VMEM((len(PAIRS), 8, 128), f32)],
+        in_specs=[vmem, vmem],
+        out_specs=(hbm, vmem),
+        scratch_shapes=[
+            pltpu.VMEM((len(PAIRS), 8, 128), f32),
+            pltpu.VMEM(forcing.shape, f32),
+            dma((NV,)),
+        ],
         compiler_params=pltpu.CompilerParams(vmem_limit_bytes=16 * 2**20),
         name="basis",
     )(gram, response))

time: 45.3 us -> 38 us (0.84)
  local copies, waits for them, and re-layouts: 6.53 us -> 0 us
  Pallas kernels: 37.9 us -> 37.3 us
    unnamed x10 -> x0, local copies, waits for them, and re-layouts: 6.53 us -> none
    pallas_call x1, Pallas kernels: 4.57 us -> 3.78 us  [local(): pl.pallas_call(basis_kernel, out_shape=(jax.ShapeDtypeStruct(forcing.shap...]
where the time goes in v2:
time: 38 us; the launch traced here: 37.9 us
  Pallas kernels  37.3 us (98%)
  between operations  0.64 us (2%)
    pallas_call x1, Pallas kernels, local(): pl.pallas_call(functools.partial(response_kernel, nx, ny), out_shape=(jax...  33.5 us
    pallas_call x1, Pallas kernels, local(): pl.pallas_call(basis_kernel, out_shape=(jax.ShapeDtypeStruct(forcing.shap...  3.78 us

profile of v2, /device:TPU:0, one launch (start us, length us, event | category | flops | bytes accessed | tf_op | source)
XLA Modules:
  0.0 37.9 jit_solution(2381721610960752809)
XLA Ops:
  0.6 33.5 %response.1 = (f32[4,8,256,128]{3,2,1,0:T(8,128)S(1)}, f32[8,128]{1,0:T(8,128)S(1)}) custom-call(f32[4,8,256,128]{3,2,1,0:T(8,128)} %f_hbm.1, f32[2,256,128]{2,1,0:T(8,128)} %vel_hbm.1, f32[256,128]{1,0:T(8,128)} %visc_hbm.1, f32[256,128]{1,0:T(8,128)} %sound_hbm.1, f32[4,4,256,128]{3,2,1,0:T(8,128)} %coup_hbm.1), custom_call_target="tpu_custom_call" | custom-call | tf_op jit(solution)/shard_map/response/pallas_call | solution.py:345
  34.1 3.8 %basis.1 = (f32[4,8,256,128]{3,2,1,0:T(8,128)}, f32[8,8]{1,0:T(8,128)}) custom-call(f32[8,128]{1,0:T(8,128)S(1)} %get-tuple-element.4.gram_ref, f32[4,8,256,128]{3,2,1,0:T(8,128)S(1)} %get-tuple-element.5.r_ref), custom_call_target="tpu_custom_call" | custom-call | tf_op jit(solution)/shard_map/basis/pallas_call | solution.py:378
